TPU v7x, 512 devices: a whole 4x4x16 slice. The times are simulated.
512 devices in a mesh: row: 8 (over z_lo), col: 8 (over z_hi, y), depth: 8 (over x, core).
Axes of the slice: x: 4, y: 4, z: 16 (z_hi: 2, z_lo: 8; z = z_hi * 8 + z_lo), core: 2. Of those that a mesh axis runs over, the one named last changes fastest.
Arguments:
- tile_values: bfloat16 [8, 64, 64, 128, 128], P('row', ('col', 'depth')), may hold values from 0 to 0.019897461
- tile_rows: int32 [8, 64, 64], P('row', ('col', 'depth')), may hold values from 0 to 39, as said below
- tile_cols: int32 [8, 64, 64], P('row', ('col', 'depth')), may hold values from 0 to 4
- tile_count: int32 [8, 64], P('row', ('col', 'depth')), may hold values from 1 to 64, as said below
- features: bfloat16 [40960, 128], P(('col', 'depth')), may hold values from -6 to 6
- weight: bfloat16 [128, 256], replicated, may hold values from -0.5 to 0.5
- cotangent: bfloat16 [40960, 256], P(('row', 'col', 'depth')), may hold values from -6 to 6
Outputs:
- activations: bfloat16 [40960, 256], P(('row', 'col', 'depth'))
- input_grad: bfloat16 [64, 640, 128], P(('col', 'depth'), 'row')
- weight_grad: float32 [128, 256], replicated
Inputs may be any that keep to these rules, and one draw needn't show every extreme that they name: Within one device the pairs (tile_rows, tile_cols) of all 64 slots are distinct. `tile_count`: some device holds 64 tiles in every draw.
All inputs are finite; a program needn't handle non-finite values.
Results may differ from a plain program's by a relative error of at most 0.019.
Values may be sent and summed in bfloat16 or wider, within the bound.
A program may use at most 64 MiB of HBM per device.

v0:
```python
import math

import jax
import jax.numpy as jnp
from jax import lax
from jax.sharding import PartitionSpec as P

TILE = 128
RB = 40


def silu_slope(pre):
    sig = jax.nn.sigmoid(pre)
    return sig * (1.0 + pre * (1.0 - sig))


def local(tile_values, tile_rows, tile_cols, tile_count, features, weight, cotangent):
    values = tile_values[0, 0]
    rows = tile_rows[0, 0]
    cols = tile_cols[0, 0]
    slots = jnp.arange(rows.shape[0], dtype=jnp.int32)
    live = slots < tile_count[0, 0]
    col_blocks = features.shape[0] // TILE
    slab_rows = RB * TILE
    row_target = jnp.where(live, rows, RB)
    col_target = jnp.where(live, cols, col_blocks)
    nodes = slab_rows * lax.axis_size("row")
    padded = jnp.zeros((RB + 1, col_blocks + 1, TILE, TILE), jnp.bfloat16)
    padded = padded.at[row_target, col_target].set(values)
    dense = padded[:RB, :col_blocks].transpose(0, 2, 1, 3).reshape(slab_rows, col_blocks * TILE)
    partial_value = jnp.dot(dense, features, preferred_element_type=jnp.float32)
    share = lax.psum_scatter(partial_value, ("col", "depth"), scatter_dimension=0, tiled=True)
    agg = share.astype(jnp.bfloat16)
    pre = jnp.dot(agg, weight, preferred_element_type=jnp.float32)
    activations = jax.nn.silu(pre).astype(jnp.bfloat16)
    grad_pre = (cotangent.astype(jnp.float32) * silu_slope(pre)).astype(jnp.bfloat16)
    local_terms = jnp.einsum("nf,nh->fh", agg, grad_pre, preferred_element_type=jnp.float32)
    weight_grad = lax.psum(local_terms, ("row", "col", "depth"))
    grad_agg = jnp.einsum("nh,fh->nf", grad_pre, weight, preferred_element_type=jnp.float32).astype(
        jnp.bfloat16
    )
    grad_slab = lax.all_gather(grad_agg, ("col", "depth"), axis=0, tiled=True)
    weight_grad = weight_grad / math.sqrt(nodes)
    inner = jnp.einsum("nc,nf->cf", dense, grad_slab, preferred_element_type=jnp.float32)
    input_grad = lax.psum_scatter(
        inner.astype(jnp.bfloat16), "row", scatter_dimension=0, tiled=True
    )
    return (activations, input_grad[None], weight_grad)


def solution(mesh):
    in_specs = (
        P("row", ("col", "depth"), None, None, None),
        P("row", ("col", "depth"), None),
        P("row", ("col", "depth"), None),
        P("row", ("col", "depth")),
        P(("col", "depth"), None),
        P(),
        P(("row", "col", "depth"), None),
    )
    out_specs = (P(("row", "col", "depth"), None), P(("col", "depth"), "row", None), P())
    return jax.shard_map(local, mesh=mesh, in_specs=in_specs, out_specs=out_specs, check_vma=False)
```

profile of v0, /device:TPU:1, one launch (start us, length us, event | category | flops | bytes accessed | tf_op | source)
XLA Modules:
  0.0 1233.0 jit_solution(5628599662302898750)
XLA Ops:
  7.2 0.0 copy-start
  7.2 0.0 copy-start.1
  7.2 0.0 reduce-scatter.3.cloned.1.call-start
  8.0 0.7 fusion.14
  8.7 5.1 broadcast_in_dim.15
  13.9 0.0 copy-done.1
  13.9 10.9 scatter_fusion
  24.8 8.4 slice_bitcast_fusion
  33.2 10.7 copy.10
  44.0 0.0 copy-done
  44.0 0.0 copy-start.2
  44.0 0.0 copy-start.3
  44.0 6.4 fusion.2
  50.3 0.0 reduce-scatter.3.cloned.1.call-update
  50.4 0.0 all-gather.2.cloned.1.call-start
  50.4 567.8 %reduce-scatter.3.cloned.1.call-done = f32[80,128]{1,0:T(8,128)} async-done(((f32[5120,128]{1,0:T(8,128)}), f32[80,128]{1,0:T(8,128)}) %reduce-scatter.3.cloned.1.call-update) | async-done | bytes 40976 | tf_op jit(solution)/shard_map/reduce_scatter | solution.py:32
  618.2 0.0 copy-done.2
  618.2 0.0 copy-done.3
  618.2 1.6 multiply_convert_fusion
  619.8 0.8 convolution_convert_fusion
  620.6 0.0 all-gather.2.cloned.1.call-update
  620.6 0.0 all-reduce.2.cloned.1.call-start
  620.6 1.6 fusion.9
  622.3 0.0 all-reduce.2.cloned.1.call-update
  622.3 0.0 reduce-scatter.5.cloned.1.call-start
  622.4 109.1 %all-gather.2.cloned.1.call-done = bf16[5120,128]{1,0:T(8,128)(2,1)} async-done(((bf16[80,128]{1,0:T(8,128)(2,1)}), bf16[5120,128]{1,0:T(8,128)(2,1)}) %all-gather.2.cloned.1.call-update) | async-done | bytes 1310736 | tf_op jit(solution)/shard_map/all_gather | solution.py:42
  731.5 5.7 fusion.6
  737.2 0.0 reduce-scatter.5.cloned.1.call-update
  737.2 438.2 %all-reduce.2.cloned.1.call-done = f32[128,256]{1,0:T(8,128)} async-done(((f32[128,256]{1,0:T(8,128)}), f32[128,256]{1,0:T(8,128)}) %all-reduce.2.cloned.1.call-update) | async-done | bytes 131088 | tf_op jit(solution)/shard_map/psum | solution.py:38
  1175.5 1.6 broadcast_multiply_fusion
  1177.0 49.5 %reduce-scatter.5.cloned.1.call-done = bf16[80,128]{1,0:T(8,128)(2,1)} async-done(((bf16[640,128]{1,0:T(8,128)(2,1)}), bf16[80,128]{1,0:T(8,128)(2,1)}) %reduce-scatter.5.cloned.1.call-update) | async-done | bytes 20496 | tf_op jit(solution)/shard_map/reduce_scatter | solution.py:45
Async XLA Ops:
  7.2 36.8 %copy-start = (bf16[640,128]{1,0:T(8,128)(2,1)S(1)}, bf16[640,128]{1,0:T(8,128)(2,1)}, u32[]{:S(2)}) copy-start(bf16[640,128]{1,0:T(8,128)(2,1)} %param.11) | copy-start | bytes 491524
  7.2 6.7 copy-start.1
  7.2 611.0 %reduce-scatter.3.cloned.1.call-start = ((), (), s32[]{:S(2)}) async-start(), calls=%async_computation.2 | async-start | bytes 2662400 | tf_op jit(solution)/shard_map/reduce_scatter | solution.py:32
  44.0 574.3 %copy-start.2 = (bf16[128,256]{1,0:T(8,128)(2,1)S(1)}, bf16[128,256]{1,0:T(8,128)(2,1)}, u32[]{:S(2)}) copy-start(bf16[128,256]{1,0:T(8,128)(2,1)} %param.12) | copy-start | bytes 196612
  44.0 574.3 %copy-start.3 = (bf16[80,256]{1,0:T(8,128)(2,1)S(1)}, bf16[80,256]{1,0:T(8,128)(2,1)}, u32[]{:S(2)}) copy-start(bf16[80,256]{1,0:T(8,128)(2,1)} %param.13) | copy-start | bytes 122884
  50.4 681.1 %all-gather.2.cloned.1.call-start = ((), (), s32[]{:S(2)}) async-start(), calls=%async_computation.3 | async-start | bytes 1331200 | tf_op jit(solution)/shard_map/all_gather | solution.py:42
  620.6 554.9 %all-reduce.2.cloned.1.call-start = ((), (), s32[]{:S(2)}) async-start(), calls=%async_computation.5 | async-start | bytes 262144 | tf_op jit(solution)/shard_map/psum | solution.py:38
  622.3 604.2 %reduce-scatter.5.cloned.1.call-start = ((), (), s32[]{:S(2)}) async-start(), calls=%async_computation.4 | async-start | bytes 184320 | tf_op jit(solution)/shard_map/reduce_scatter | solution.py:45
Sparse Core Ops, SparseCore 0:
  50.5 567.7 reduce-scatter.2
  624.0 107.3 all-gather.1
  738.4 437.0 all-reduce.1
  1178.7 47.7 reduce-scatter.4
where the time goes:
time: 1240 us; the launch traced here: 1230 us
  waiting for transfers between devices  1160 us (94%)
  local copies, waits for them, and re-layouts  35.3 us (3%)
  matrix products  16.1 us (1%)
  between operations  14.6 us (1%)
    reduce_scatter x1, waiting for transfers between devices, local(): lax.psum_scatter(partial_value, ('col', 'depth'), scatter_dimension=0, ti...  568 us
    psum x1, waiting for transfers between devices, local(): weight_grad = lax.psum(local_terms, ('row', 'col', 'depth'))  438 us
    all_gather x1, waiting for transfers between devices, local(): grad_slab = lax.all_gather(grad_agg, ('col', 'depth'), axis=0, tiled=True)  109 us
    reduce_scatter x1, waiting for transfers between devices, local(): lax.psum_scatter(inner.astype(jnp.bfloat16), 'row', scatter_dimension=0,...  49.5 us
  transfers between devices with their start and end apart: 4, of which 4 were waited for; matrix products, arithmetic and copies ran while one was open for 1% of the time, Pallas kernels for 0%

commit v1 on v0

v1 whole, which is shorter than its diff:
```python
import functools
import math

import jax
import jax.numpy as jnp
from jax import lax
from jax.experimental import pallas as pl
from jax.experimental.pallas import tpu as pltpu
from jax.sharding import PartitionSpec as P

TILE = 128
Z_HI = 2
CORES = 2
BF16 = jnp.bfloat16
F32 = jnp.float32


def kernel(
    sizes, table, vals_in, feat_in, w_in, cot_in, act_out, ig_out, wg_out,
    vals, valst, feat, w, cot, act, part, sb, rb, qs, own, slots, zsend, zrecv, g, acc,
    xs, xr, ig, wt, wr, wslots, wz, wsend, wrecv, wo,
    load_sem, out_sem, s1s, s1r, s2s, s2r, zsem, ga_s, ga_r, gp_r, gc_s, gc_r,
    xsem, w1, w2, w3, w4, w5, w6,
):
    n_row, n_y, n_x, ch, n_cb, block_tiles, slots_max = sizes
    n_blocks = Z_HI * n_y
    plane = n_x * n_y
    zc = n_cb * TILE // n_row
    row, col, depth = lax.axis_index("row"), lax.axis_index("col"), lax.axis_index("depth")
    zh, y = lax.div(col, n_y), lax.rem(col, n_y)
    x, core = lax.div(depth, CORES), lax.rem(depth, CORES)
    z_other, other = 1 - zh, 1 - core
    here = y * n_x + x

    sibling = (row, col, x * CORES + other)
    partner = (row, z_other * n_y + y, depth)

    def in_plane(dy, dx):
        yy, xx = lax.rem(y + dy, n_y), lax.rem(x + dx, n_x)
        return yy, xx, (row, zh * n_y + yy, xx * CORES + core)

    def in_row(dz):
        rr = lax.rem(row + dz, n_row)
        return rr, (rr, col, depth)

    offsets = [(dy, dx) for dy in range(n_y) for dx in range(n_x) if (dy, dx) != (0, 0)]

    def send(src, dst, send_sem, recv_sem, device):
        pltpu.make_async_remote_copy(
            src_ref=src, dst_ref=dst, send_sem=send_sem, recv_sem=recv_sem,
            device_id=device, device_id_type=pl.DeviceIdType.MESH,
        ).start()

    def wait(ref, sem):
        pltpu.make_async_copy(ref, ref, sem).wait()

    loads = [
        pltpu.make_async_copy(feat_in, feat, load_sem.at[0]),
        pltpu.make_async_copy(vals_in.at[0, 0], vals.at[pl.ds(0, slots_max)], load_sem.at[1]),
        pltpu.make_async_copy(w_in, w, load_sem.at[2]),
        pltpu.make_async_copy(cot_in, cot, load_sem.at[3]),
    ]
    for load in loads:
        load.start()

    barrier = pltpu.get_barrier_semaphore()
    peers = [sibling, partner]
    peers += [in_plane(dy, dx)[2] for dy, dx in offsets]
    peers += [in_row(dz)[1] for dz in range(1, n_row)]
    for peer in peers:
        pl.semaphore_signal(barrier, inc=1, device_id=peer, device_id_type=pl.DeviceIdType.MESH)

    vals[slots_max] = jnp.zeros((TILE, TILE), BF16)
    valst[slots_max] = jnp.zeros((TILE, TILE), BF16)
    loads[0].wait()
    loads[1].wait()
    pl.semaphore_wait(barrier, len(peers))

    def place(j):
        phase, dy = lax.div(j, n_y), lax.rem(j + 1, n_y)
        z = lax.rem(zh + 1 + phase, Z_HI)
        return phase, dy, z * n_y + lax.rem(y + dy, n_y)

    def chunk(b, xx, cc):
        return part[b, pl.ds(pl.multiple_of((xx * CORES + cc) * ch, 16), ch), :]

    def forward(j, carry):
        @pl.when(j < n_blocks)
        def _():
            _, _, b = place(j)
            for i in range(block_tiles):
                at = (b * block_tiles + i) * n_cb
                lhs = jnp.concatenate([vals[table[at + c]] for c in range(n_cb)], axis=1)
                part[b, i * TILE : (i + 1) * TILE, :] = jnp.dot(
                    lhs, feat[...], preferred_element_type=F32
                )
            for xx in range(n_x):
                sb[b, xx] = chunk(b, xx, other).astype(BF16)
            send(sb.at[b], rb.at[b], s1s, s1r.at[b], sibling)

        @pl.when(j > 0)
        def _():
            phase, dy, b = place(j - 1)
            wait(rb.at[b], s1r.at[b])
            for dx in range(n_x):
                yy, xx, device = in_plane(dy, dx)
                total = chunk(b, xx, core) + rb[b, xx].astype(F32)
                qs[b, xx] = total.astype(BF16)
                slot = dy * n_x + dx
                if dx == 0:

                    @pl.when(dy == 0)
                    def _():
                        own[phase] = total

                    @pl.when(dy != 0)
                    def _():
                        send(qs.at[b, xx], slots.at[phase, slot], s2s, s2r.at[phase], device)
                else:
                    send(qs.at[b, xx], slots.at[phase, slot], s2s, s2r.at[phase], device)

        return carry

    lax.fori_loop(0, n_blocks + 1, forward, 0)

    def plane_sum(phase):
        wait(slots.at[phase, pl.ds(1, plane - 1)], s2r.at[phase])
        return lax.fori_loop(
            1, plane, lambda k, t: t + slots[phase, k].astype(F32), own[phase]
        )

    zsend[...] = plane_sum(0).astype(BF16)
    send(zsend, zrecv, zsem.at[0], zsem.at[1], partner)

    def turn(t, carry):
        valst[t] = vals[t].T
        return carry

    lax.fori_loop(0, slots_max, turn, 0)
    total = plane_sum(1)
    loads[2].wait()
    loads[3].wait()
    wait(zrecv, zsem.at[1])
    agg = (total + zrecv[...].astype(F32)).astype(BF16)

    pre = jnp.dot(agg, w[...], preferred_element_type=F32)
    sig = jax.nn.sigmoid(pre)
    act[...] = (pre * sig).astype(BF16)
    slope = sig * (1.0 + pre * (1.0 - sig))
    grad_pre = (cot[...].astype(F32) * slope).astype(BF16)
    grad_agg = lax.dot_general(
        grad_pre, w[...], (((1,), (1,)), ((), ())), preferred_element_type=F32
    ).astype(BF16)
    g[col, x, core] = grad_agg

    b_here = z_other * n_y + y
    mine = g.at[col, x, core]
    send(mine, mine, ga_s, gp_r, partner)
    for dy, dx in offsets:
        send(mine, mine, ga_s, ga_r.at[0, dy], in_plane(dy, dx)[2])

    terms = lax.dot_general(agg, grad_pre, (((0,), (0,)), ((), ())), preferred_element_type=F32)
    wt[0] = terms[:, :TILE].reshape(wt.shape[1:])
    wt[1] = terms[:, TILE:].reshape(wt.shape[1:])
    send(wt.at[other], wr, w1.at[0], w1.at[1], sibling)
    act_copy = pltpu.make_async_copy(act, act_out, out_sem.at[0])
    act_copy.start()

    acc[...] = jnp.zeros_like(acc)

    def pass_on(phase, dy):
        z = lax.rem(zh + phase, Z_HI)
        b = z * n_y + lax.rem(y + n_y - dy, n_y)
        if dy == 0:
            wait(slots.at[0, pl.ds(0, n_x - 1)], ga_r.at[phase, dy])
        else:
            wait(g.at[b, pl.ds(0, n_x), core], ga_r.at[phase, dy])
        group = g.at[b, pl.ds(0, n_x), core]
        send(group, group, gc_s, gc_r.at[phase, dy], sibling)

    def backward(phase):
        def step(dy, carry):
            z = lax.rem(zh + phase, Z_HI)
            b = z * n_y + lax.rem(y + n_y - dy, n_y)
            wait(g.at[b, pl.ds(0, n_x), other], gc_r.at[phase, dy])
            grad = g[b].reshape(block_tiles * TILE, TILE)
            for c in range(n_cb):
                at = b * block_tiles * n_cb + c
                lhs = jnp.concatenate(
                    [valst[table[at + i * n_cb]] for i in range(block_tiles)], axis=1
                )
                acc[c * TILE : (c + 1) * TILE, :] += jnp.dot(
                    lhs, grad, preferred_element_type=F32
                )
            return carry

        lax.fori_loop(0, n_y, step, 0)

    wait(g.at[b_here, x, core], gp_r)
    theirs = g.at[b_here, x, core]
    for dy, dx in offsets:
        send(theirs, theirs, ga_s, ga_r.at[1, dy], in_plane(dy, dx)[2])
    wait(wr, w1.at[1])
    wt[core] = wt[core] + wr[...]
    for dy, dx in offsets:
        yy, xx, device = in_plane(dy, dx)
        send(wt.at[core, yy * n_x + xx], wslots.at[dy * n_x + dx], w2.at[0], w2.at[1], device)

    for dy in range(n_y):
        pass_on(0, dy)
    wait(wslots.at[pl.ds(1, plane - 1)], w2.at[1])
    wz[row] = lax.fori_loop(1, plane, lambda k, t: t + wslots[k], wt[core, here])
    for dz in range(1, n_row):
        send(wz.at[row], wz.at[row], w3.at[0], w3.at[1], in_row(dz)[1])

    backward(0)
    for dy in range(n_y):
        pass_on(1, dy)
    wait(wz.at[pl.ds(0, n_row - 1)], w3.at[1])
    wsend[...] = lax.fori_loop(1, n_row, lambda k, t: t + wz[k], wz[0])
    send(wsend, wrecv, w4.at[0], w4.at[1], partner)

    backward(1)
    for d in range(n_row):
        xs[d] = acc[d * zc : (d + 1) * zc, :].astype(BF16)
    for dz in range(1, n_row):
        rr, device = in_row(dz)
        send(xs.at[rr], xr.at[dz], xsem.at[0], xsem.at[1], device)

    scale = 1.0 / math.sqrt(n_row * n_blocks * block_tiles * TILE)
    wait(wrecv, w4.at[1])
    wo[core, here] = (wsend[...] + wrecv[...]) * scale
    final = wo.at[core, here]
    for dy, dx in offsets:
        send(final, final, w5.at[0], w5.at[1], in_plane(dy, dx)[2])
    wait(wo.at[core, pl.ds(0, plane - 1)], w5.at[1])
    send(wo.at[core], wo.at[core], w6.at[0], w6.at[1], sibling)

    inner = acc[pl.ds(pl.multiple_of(row * zc, 16), zc), :]
    wait(xr.at[pl.ds(1, n_row - 1)], xsem.at[1])
    ig[...] = lax.fori_loop(1, n_row, lambda k, t: t + xr[k].astype(F32), inner).astype(BF16)
    ig_copy = pltpu.make_async_copy(ig, ig_out, out_sem.at[1])
    ig_copy.start()
    wait(wo.at[other], w6.at[1])
    wg_copies = [
        pltpu.make_async_copy(wo.at[c], wg_out.at[c], out_sem.at[2 + c]) for c in range(CORES)
    ]
    for copy in wg_copies:
        copy.start()

    wait(sb, s1s)
    wait(slots.at[:, pl.ds(1, plane - 1)], s2s)
    wait(zsend, zsem.at[0])
    wait(slots.at[0], ga_s)
    wait(slots.at[0, pl.ds(1, plane - 1)], ga_s)
    wait(sb, gc_s)
    wait(wt.at[other], w1.at[0])
    wait(wslots.at[pl.ds(1, plane - 1)], w2.at[0])
    wait(wz.at[pl.ds(0, n_row - 1)], w3.at[0])
    wait(wsend, w4.at[0])
    wait(wo.at[core, pl.ds(0, plane - 1)], w5.at[0])
    wait(wo.at[core], w6.at[0])
    wait(xr.at[pl.ds(1, n_row - 1)], xsem.at[0])
    for copy in [act_copy, ig_copy] + wg_copies:
        copy.wait()


def local(tile_values, tile_rows, tile_cols, tile_count, features, weight, cotangent):
    n_row, n_col, n_depth = lax.axis_size("row"), lax.axis_size("col"), lax.axis_size("depth")
    n_y, n_x = n_col // Z_HI, n_depth // CORES
    ch, hid = cotangent.shape
    f = features.shape[1]
    n_cb = features.shape[0] // TILE
    n_blocks = n_col
    block_rows = n_depth * ch
    block_tiles = block_rows // TILE
    n_tiles = n_blocks * block_tiles
    slots_max = tile_values.shape[2]
    plane = n_x * n_y
    zc = features.shape[0] // n_row
    piece = f // plane

    slot = jnp.arange(slots_max, dtype=jnp.int32)
    key = jnp.where(slot < tile_count[0, 0], tile_rows[0, 0] * n_cb + tile_cols[0, 0], -1)
    where_at = jnp.arange(n_tiles * n_cb, dtype=jnp.int32)
    table = jnp.min(
        jnp.where(key[:, None] == where_at[None, :], slot[:, None], slots_max), axis=0
    )

    sizes = (n_row, n_y, n_x, ch, n_cb, block_tiles, slots_max)
    vmem, dma = pltpu.VMEM, pltpu.SemaphoreType.DMA
    anywhere = pl.BlockSpec(memory_space=pl.ANY)
    act, ig, wg = pl.pallas_call(
        functools.partial(kernel, sizes),
        out_shape=(
            jax.ShapeDtypeStruct((ch, hid), BF16),
            jax.ShapeDtypeStruct((zc, f), BF16),
            jax.ShapeDtypeStruct((CORES, plane, piece, TILE), F32),
        ),
        in_specs=[pl.BlockSpec(memory_space=pltpu.SMEM)] + [anywhere] * 4,
        out_specs=(anywhere,) * 3,
        scratch_shapes=[
            vmem((slots_max + 1, TILE, TILE), BF16),
            vmem((slots_max + 1, TILE, TILE), BF16),
            vmem(features.shape, BF16),
            vmem(weight.shape, BF16),
            vmem((ch, hid), BF16),
            vmem((ch, hid), BF16),
            vmem((n_blocks, block_rows, f), F32),
            vmem((n_blocks, n_x, ch, f), BF16),
            vmem((n_blocks, n_x, ch, f), BF16),
            vmem((n_blocks, n_x, ch, f), BF16),
            vmem((Z_HI, ch, f), F32),
            vmem((Z_HI, plane, ch, f), BF16),
            vmem((ch, f), BF16),
            vmem((ch, f), BF16),
            vmem((n_blocks, n_x, CORES, ch, f), BF16),
            vmem((n_cb * TILE, f), F32),
            vmem((n_row, zc, f), BF16),
            vmem((n_row, zc, f), BF16),
            vmem((zc, f), BF16),
            vmem((CORES, plane, piece, TILE), F32),
            vmem((plane, piece, TILE), F32),
            vmem((plane, piece, TILE), F32),
            vmem((n_row, piece, TILE), F32),
            vmem((piece, TILE), F32),
            vmem((piece, TILE), F32),
            vmem((CORES, plane, piece, TILE), F32),
            dma((4,)),
            dma((4,)),
            dma,
            dma((n_blocks,)),
            dma,
            dma((Z_HI,)),
            dma((2,)),
            dma,
            dma((Z_HI, n_y)),
            dma,
            dma,
            dma((Z_HI, n_y)),
            dma((2,)),
            dma((2,)),
            dma((2,)),
            dma((2,)),
            dma((2,)),
            dma((2,)),
            dma((2,)),
        ],
        compiler_params=pltpu.CompilerParams(
            collective_id=0, has_side_effects=True, vmem_limit_bytes=40 * 1024 * 1024
        ),
        name="graph_layer",
    )(table, tile_values, features, weight, cotangent)
    weight_grad = wg.reshape(CORES, f, TILE).transpose(1, 0, 2).reshape(f, hid)
    return act, ig[None], weight_grad


def solution(mesh):
    in_specs = (
        P("row", ("col", "depth"), None, None, None),
        P("row", ("col", "depth"), None),
        P("row", ("col", "depth"), None),
        P("row", ("col", "depth")),
        P(("col", "depth"), None),
        P(),
        P(("row", "col", "depth"), None),
    )
    out_specs = (P(("row", "col", "depth"), None), P(("col", "depth"), "row", None), P())
    return jax.shard_map(local, mesh=mesh, in_specs=in_specs, out_specs=out_specs, check_vma=False)
```

time: 1240 us -> 78.1 us (0.06)
  waiting for transfers between devices: 1160 us -> 0 us
  Pallas kernels: 0 us -> 69.7 us
  local copies, waits for them, and re-layouts: 35.3 us -> 6.01 us
  matrix products: 16.1 us -> 0 us
  between operations: 14.6 us -> 1.3 us
    reduce_scatter x2 -> x0, waiting for transfers between devices: 617 us -> none  [the longest x1 568 us: local(): lax.psum_scatter(partial_value, ('col', 'depth'), scatter_dimension=0, ti...]
    psum x1 -> x0, waiting for transfers between devices: 438 us -> none  [local(): weight_grad = lax.psum(local_terms, ('row', 'col', 'depth'))]
    all_gather x1 -> x0, waiting for transfers between devices: 109 us -> none  [local(): grad_slab = lax.all_gather(grad_agg, ('col', 'depth'), axis=0, tiled=True)]
    pallas_call x0 -> x1, Pallas kernels: none -> 69.7 us  [local(): pl.pallas_call(functools.partial(kernel, sizes), out_shape=(jax.ShapeDtyp...]
    transpose x2 -> x0, local copies, waits for them, and re-layouts: 19.2 us -> none  [local(): padded[:RB, :col_blocks].transpose(0, 2, 1, 3)]
    dot_general x5 -> x0, matrix products: 16.1 us -> none  [the longest x1 6.36 us: local(): partial_value = jnp.dot(dense, features, preferred_element_type=jnp.float32)]
  transfers between devices with their start and end apart: 4 -> 0, of which waited for: 4 -> 0; matrix products, arithmetic and copies ran while one was open for 1% -> 0% of each run, Pallas kernels for 0% -> 0%
where the time goes in v1:
time: 78.1 us; the launch traced here: 77.8 us
  Pallas kernels  69.7 us (89%)
  local copies, waits for them, and re-layouts  6.01 us (8%)
  between operations  1.3 us (2%)
    pallas_call x1, Pallas kernels, local(): pl.pallas_call(functools.partial(kernel, sizes), out_shape=(jax.ShapeDtyp...  69.7 us
    unnamed x10, local copies, waits for them, and re-layouts  5.34 us

profile of v1, /device:TPU:1, one launch (start us, length us, event | category | flops | bytes accessed | tf_op | source)
XLA Modules:
  0.0 77.8 jit_solution(14849997952225127958)
XLA Ops:
  1.3 0.7 compare_select_fusion
  2.0 0.1 select_reduce_fusion.table
  2.0 0.0 copy-start
  2.1 1.6 %copy-done = bf16[1,1,64,128,128]{4,3,2,1,0:T(8,128)(2,1)S(1)} copy-done((bf16[1,1,64,128,128]{4,3,2,1,0:T(8,128)(2,1)S(1)}, bf16[1,1,64,128,128]{4,3,2,1,0:T(8,128)(2,1)}, u32[]{:S(2)}) %copy-start) | copy-done | bytes 2097176
  3.6 0.0 copy-start.1
  3.6 0.9 %copy-done.1 = bf16[640,128]{1,0:T(8,128)(2,1)S(1)} copy-done((bf16[640,128]{1,0:T(8,128)(2,1)S(1)}, bf16[640,128]{1,0:T(8,128)(2,1)}, u32[]{:S(2)}) %copy-start.1) | copy-done | bytes 163864
  4.6 0.0 copy-start.2
  4.6 0.8 %copy-done.2 = bf16[128,256]{1,0:T(8,128)(2,1)S(1)} copy-done((bf16[128,256]{1,0:T(8,128)(2,1)S(1)}, bf16[128,256]{1,0:T(8,128)(2,1)}, u32[]{:S(2)}) %copy-start.2) | copy-done | bytes 65560
  5.4 0.0 copy-start.3
  5.4 0.8 copy-done.3
  6.2 69.7 %graph_layer.1 = (bf16[80,256]{1,0:T(8,128)(2,1)S(1)}, bf16[80,128]{1,0:T(8,128)(2,1)S(1)}, f32[2,16,8,128]{3,2,1,0:T(8,128)S(1)}) custom-call(s32[200]{0:T(256)S(1)} %select_reduce_fusion.table, bf16[1,1,64,128,128]{4,3,2,1,0:T(8,128)(2,1)S(1)} %copy-done, bf16[640,128]{1,0:T(8,128)(2,1)S(1)} %copy-done.1, bf16[128,256]{1,0:T(8,128)(2,1)S(1)} %copy-done.2, ...), custom_call_target="tpu_custom_call" | custom-call | tf_op jit(solution)/shard_map/graph_layer/pallas_call | solution.py:293
  75.9 0.7 copy.14
  76.6 0.6 copy.18
  77.2 0.6 copy.19
Async XLA Ops:
  2.0 1.6 %copy-start = (bf16[1,1,64,128,128]{4,3,2,1,0:T(8,128)(2,1)S(1)}, bf16[1,1,64,128,128]{4,3,2,1,0:T(8,128)(2,1)}, u32[]{:S(2)}) copy-start(bf16[1,1,64,128,128]{4,3,2,1,0:T(8,128)(2,1)} %vals_in.1) | copy-start | bytes 6291460
  3.6 0.9 %copy-start.1 = (bf16[640,128]{1,0:T(8,128)(2,1)S(1)}, bf16[640,128]{1,0:T(8,128)(2,1)}, u32[]{:S(2)}) copy-start(bf16[640,128]{1,0:T(8,128)(2,1)} %feat_in.1) | copy-start | bytes 491524
  4.6 0.8 %copy-start.2 = (bf16[128,256]{1,0:T(8,128)(2,1)S(1)}, bf16[128,256]{1,0:T(8,128)(2,1)}, u32[]{:S(2)}) copy-start(bf16[128,256]{1,0:T(8,128)(2,1)} %w_in.1) | copy-start | bytes 196612
  5.4 0.8 %copy-start.3 = (bf16[80,256]{1,0:T(8,128)(2,1)S(1)}, bf16[80,256]{1,0:T(8,128)(2,1)}, u32[]{:S(2)}) copy-start(bf16[80,256]{1,0:T(8,128)(2,1)} %cot_in.1) | copy-start | bytes 122884

commit v2 on v1

v2 whole, which is shorter than its diff:
```python
import functools
import math

import jax
import jax.numpy as jnp
from jax import lax
from jax.experimental import pallas as pl
from jax.experimental.pallas import tpu as pltpu
from jax.sharding import PartitionSpec as P

TILE = 128
Z_HI = 2
CORES = 2
BF16 = jnp.bfloat16
F32 = jnp.float32


def kernel(
    sizes, table, cols, vals_in, feat_in, w_in, cot_in, act_out, ig_out, wg_out,
    vals, valst, feat, w, cot, act, dense, prod, part, sb, rb, qs, own, slots, zsend, zrecv, g, acc,
    xs, xr, ig, wt, wr, wslots, wz, wo,
    load_sem, out_sem, csem, s1s, s1r, s2s, s2r, zs, zr, ga_s, ga_r, gc_s, gc_r,
    xsem, w1, w2, w3, w5, w6,
):
    n_row, n_y, n_x, ch, n_cb, block_tiles, slots_max = sizes
    n_blocks = Z_HI * n_y
    plane = n_x * n_y
    zc = n_cb * TILE // n_row
    row, col, depth = lax.axis_index("row"), lax.axis_index("col"), lax.axis_index("depth")
    zh, y = lax.div(col, n_y), lax.rem(col, n_y)
    x, core = lax.div(depth, CORES), lax.rem(depth, CORES)
    z_other, other = 1 - zh, 1 - core
    here = y * n_x + x

    sibling = (row, col, x * CORES + other)
    partner = (row, z_other * n_y + y, depth)

    def in_plane(dy, dx):
        yy, xx = lax.rem(y + dy, n_y), lax.rem(x + dx, n_x)
        return yy, xx, (row, zh * n_y + yy, xx * CORES + core)

    def in_row(dz):
        rr = lax.rem(row + dz, n_row)
        return rr, (rr, col, depth)

    offsets = [(dy, dx) for dy in range(n_y) for dx in range(n_x) if (dy, dx) != (0, 0)]
    hops = lambda o: (min(o[0], n_y - o[0]), min(o[1], n_x - o[1]))
    offsets.sort(key=lambda o: (-sum(hops(o)), abs(hops(o)[0] - hops(o)[1]), o[0] + o[1]))
    first = ch // 32 * 16 + ch // 16 % 2 * 16
    pieces = [pl.ds(0, first), pl.ds(first, ch - first)]
    units = [(phase, half) for phase in range(Z_HI) for half in range(2)]
    strides = sorted(range(1, n_row), key=lambda dz: -abs(2 * dz - n_row))

    def send(src, dst, send_sem, recv_sem, device):
        pltpu.make_async_remote_copy(
            src_ref=src, dst_ref=dst, send_sem=send_sem, recv_sem=recv_sem,
            device_id=device, device_id_type=pl.DeviceIdType.MESH,
        ).start()

    def wait(ref, sem):
        pltpu.make_async_copy(ref, ref, sem).wait()

    barrier = pltpu.get_barrier_semaphore()
    peers = [sibling, partner]
    peers += [in_plane(dy, dx)[2] for dy, dx in offsets]
    peers += [in_row(dz)[1] for dz in strides]
    for peer in peers:
        pl.semaphore_signal(barrier, inc=1, device_id=peer, device_id_type=pl.DeviceIdType.MESH)

    quarter = slots_max // 4
    loads = [pltpu.make_async_copy(feat_in, feat, load_sem.at[0])]
    for q in range(4):
        span = pl.ds(q * quarter, quarter)
        loads.append(pltpu.make_async_copy(vals_in.at[0, 0, span], vals.at[span], load_sem.at[1 + q]))
    late_loads = [
        pltpu.make_async_copy(cot_in, cot.at[zh], load_sem.at[5]),
        pltpu.make_async_copy(w_in, w, load_sem.at[6]),
    ]
    for load in loads + late_loads:
        load.start()

    valst[slots_max] = jnp.zeros((TILE, TILE), BF16)
    prod[slots_max] = jnp.zeros((TILE, TILE), F32)
    for load in loads:
        load.wait()

    def multiply(t, carry):
        for u in range(4):
            s = 4 * t + u
            prod[s] = jnp.dot(vals[s], feat[cols[s]], preferred_element_type=F32)
        return carry

    lax.fori_loop(0, slots_max // 4, multiply, 0)

    def chunk(b, xx, cc):
        return part[b, pl.ds(pl.multiple_of((xx * CORES + cc) * ch, 16), ch), :]

    def gather_products(b, carry):
        for i in range(block_tiles):
            at = (b * block_tiles + i) * n_cb
            total = prod[table[at]]
            for c in range(1, n_cb):
                total = total + prod[table[at + c]]
            part[b, i * TILE : (i + 1) * TILE, :] = total
        for xx in range(n_x):
            sb[b, xx] = chunk(b, xx, other).astype(BF16)
        return carry

    lax.fori_loop(0, n_blocks, gather_products, 0)
    pl.semaphore_wait(barrier, len(peers))
    for b in range(n_blocks):
        send(sb.at[b], rb.at[b], s1s, s1r.at[b], sibling)
    for load in late_loads:
        load.wait()
    send(cot.at[zh], cot.at[zh], csem.at[0], csem.at[1], partner)

    for phase in range(Z_HI):

        def pair(yy, carry):
            b = phase * n_y + yy
            wait(rb.at[b], s1r.at[b])
            for xx in range(n_x):
                qs[b, xx] = (chunk(b, xx, core) + rb[b, xx].astype(F32)).astype(BF16)
            return carry

        lax.fori_loop(0, n_y, pair, 0)
        for half, rows in enumerate(pieces):
            for dy, dx in offsets:
                yy, xx, device = in_plane(dy, dx)
                send(
                    qs.at[phase * n_y + yy, xx, rows], slots.at[phase, dy * n_x + dx, rows],
                    s2s, s2r.at[phase, half], device,
                )
        b = phase * n_y + y
        own[phase] = chunk(b, x, core) + rb[b, x].astype(F32)

    for phase, half in units:
        rows = pieces[half]
        wait(slots.at[phase, pl.ds(1, plane - 1), rows], s2r.at[phase, half])
        total = own[phase, rows]
        for k in range(1, plane):
            total = total + slots[phase, k, rows].astype(F32)
        zsend[phase, rows] = total.astype(BF16)
        mine = zsend.at[phase, rows]
        send(mine, zrecv.at[phase, rows], zs, zr.at[phase, half], partner)

    def turn(t, carry):
        valst[t] = vals[t].T
        return carry

    lax.fori_loop(0, slots_max, turn, 0)
    wait(cot.at[z_other], csem.at[1])

    for phase, half in units:
        rows = pieces[half]
        wait(zrecv.at[phase, rows], zr.at[phase, half])
        agg = (zsend[phase, rows].astype(F32) + zrecv[phase, rows].astype(F32)).astype(BF16)
        pre = jnp.dot(agg, w[...], preferred_element_type=F32)
        sig = jax.nn.sigmoid(pre)
        slope = sig * (1.0 + pre * (1.0 - sig))
        grad_pre = (cot[phase, rows].astype(F32) * slope).astype(BF16)
        grad_agg = lax.dot_general(
            grad_pre, w[...], (((1,), (1,)), ((), ())), preferred_element_type=F32
        )
        mine = g.at[phase * n_y + y, x, core, rows]
        mine[...] = grad_agg.astype(BF16)
        for dy, dx in offsets:
            send(mine, mine, ga_s, ga_r.at[phase, half, dy], in_plane(dy, dx)[2])
        act[phase, rows] = (pre * sig).astype(BF16)
        terms = lax.dot_general(
            agg, grad_pre, (((0,), (0,)), ((), ())), preferred_element_type=F32
        )
        for lane in range(CORES):
            term = terms[:, lane * TILE : (lane + 1) * TILE].reshape(wt.shape[1:])
            wt[lane] = term if (phase, half) == (0, 0) else wt[lane] + term
    send(wt.at[other], wr, w1.at[0], w1.at[1], sibling)
    act_copy = pltpu.make_async_copy(act.at[zh], act_out, out_sem.at[0])
    act_copy.start()

    wait(wr, w1.at[1])
    wt[core] = wt[core] + wr[...]
    for dy, dx in offsets:
        yy, xx, device = in_plane(dy, dx)
        send(wt.at[core, yy * n_x + xx], wslots.at[dy * n_x + dx], w2.at[0], w2.at[1], device)

    acc[...] = jnp.zeros_like(acc)

    def gather(phase):
        def source(i):
            dy = i + lax.div(i, 2) * (5 - 2 * i)
            return dy, phase * n_y + lax.rem(y + n_y - dy, n_y)

        def step(i, carry):
            @pl.when(i < n_y)
            def _():
                dy, b = source(i)
                group = g.at[b, pl.ds(0, n_x), core]

                for half, rows in enumerate(pieces):

                    @pl.when(dy == 0)
                    def _():
                        wait(slots.at[0, pl.ds(0, n_x - 1), rows], ga_r.at[phase, half, dy])

                    @pl.when(dy != 0)
                    def _():
                        wait(g.at[b, pl.ds(0, n_x), core, rows], ga_r.at[phase, half, dy])

                send(group, group, gc_s, gc_r.at[phase, dy], sibling)

            @pl.when(i > 0)
            def _():
                dy, b = source(i - 1)
                wait(g.at[b, pl.ds(0, n_x), other], gc_r.at[phase, dy])
                for c in range(n_cb):
                    for t in range(block_tiles):
                        slot = table[(b * block_tiles + t) * n_cb + c]
                        dense[c * TILE : (c + 1) * TILE, t * TILE : (t + 1) * TILE] = valst[slot]
                grad = g[b].reshape(block_tiles * TILE, TILE)
                acc[...] += jnp.dot(dense[...], grad, preferred_element_type=F32)

            return carry

        lax.fori_loop(0, n_y + 1, step, 0)

    gather(0)
    wait(wslots.at[pl.ds(1, plane - 1)], w2.at[1])
    piece = wt[core, here]
    for k in range(1, plane):
        piece = piece + wslots[k]
    wz[row] = piece
    for dz in strides:
        send(wz.at[row], wz.at[row], w3.at[0], w3.at[1], in_row(dz)[1])

    gather(1)
    for d in range(n_row):
        xs[d] = acc[d * zc : (d + 1) * zc, :].astype(BF16)
    for dz in strides:
        rr, device = in_row(dz)
        send(xs.at[rr], xr.at[dz], xsem.at[0], xsem.at[1], device)

    wait(wz.at[pl.ds(0, n_row - 1)], w3.at[1])
    piece = wz[0]
    for k in range(1, n_row):
        piece = piece + wz[k]
    scale = 1.0 / math.sqrt(n_row * n_blocks * block_tiles * TILE)
    final = wo.at[core, here]
    final[...] = piece * scale
    for dy, dx in offsets:
        send(final, final, w5.at[0], w5.at[1], in_plane(dy, dx)[2])
    wait(wo.at[core, pl.ds(0, plane - 1)], w5.at[1])
    send(wo.at[core], wo.at[core], w6.at[0], w6.at[1], sibling)

    total = acc[pl.ds(pl.multiple_of(row * zc, 16), zc), :]
    wait(xr.at[pl.ds(1, n_row - 1)], xsem.at[1])
    for k in range(1, n_row):
        total = total + xr[k].astype(F32)
    ig[...] = total.astype(BF16)
    ig_copy = pltpu.make_async_copy(ig, ig_out, out_sem.at[1])
    ig_copy.start()
    wait(wo.at[other], w6.at[1])
    wg_copies = [
        pltpu.make_async_copy(wo.at[c], wg_out.at[c], out_sem.at[2 + c]) for c in range(CORES)
    ]
    for copy in wg_copies:
        copy.start()

    wait(sb, s1s)
    wait(cot.at[zh], csem.at[0])
    wait(slots.at[:, pl.ds(1, plane - 1)], s2s)
    wait(zsend, zs)
    wait(slots.at[:, pl.ds(1, plane - 1)], ga_s)
    wait(sb, gc_s)
    wait(wt.at[other], w1.at[0])
    wait(wslots.at[pl.ds(1, plane - 1)], w2.at[0])
    wait(wz.at[pl.ds(0, n_row - 1)], w3.at[0])
    wait(wo.at[core, pl.ds(0, plane - 1)], w5.at[0])
    wait(wo.at[core], w6.at[0])
    wait(xr.at[pl.ds(1, n_row - 1)], xsem.at[0])
    for copy in [act_copy, ig_copy] + wg_copies:
        copy.wait()


def local(tile_values, tile_rows, tile_cols, tile_count, features, weight, cotangent):
    n_row, n_col, n_depth = lax.axis_size("row"), lax.axis_size("col"), lax.axis_size("depth")
    n_y, n_x = n_col // Z_HI, n_depth // CORES
    ch, hid = cotangent.shape
    f = features.shape[1]
    n_cb = features.shape[0] // TILE
    n_blocks = n_col
    block_rows = n_depth * ch
    block_tiles = block_rows // TILE
    n_tiles = n_blocks * block_tiles
    slots_max = tile_values.shape[2]
    plane = n_x * n_y
    zc = features.shape[0] // n_row
    piece = f // plane

    slot = jnp.arange(slots_max, dtype=jnp.int32)
    key = jnp.where(slot < tile_count[0, 0], tile_rows[0, 0] * n_cb + tile_cols[0, 0], -1)
    where_at = jnp.arange(n_tiles * n_cb, dtype=jnp.int32)
    table = jnp.min(
        jnp.where(key[:, None] == where_at[None, :], slot[:, None], slots_max), axis=0
    )

    sizes = (n_row, n_y, n_x, ch, n_cb, block_tiles, slots_max)
    vmem, dma = pltpu.VMEM, pltpu.SemaphoreType.DMA
    operands = [
        pltpu.with_memory_space_constraint(a, pltpu.HBM)
        for a in (tile_values, features.reshape(n_cb, TILE, f), weight, cotangent)
    ]
    anywhere = pl.BlockSpec(memory_space=pl.ANY)
    act, ig, wg = pl.pallas_call(
        functools.partial(kernel, sizes),
        out_shape=(
            vmem((ch, hid), BF16),
            vmem((zc, f), BF16),
            vmem((CORES, plane, piece, TILE), F32),
        ),
        in_specs=[pl.BlockSpec(memory_space=pltpu.SMEM)] * 2
        + [pl.BlockSpec(memory_space=pltpu.HBM)] * 4,
        out_specs=(anywhere,) * 3,
        scratch_shapes=[
            vmem((slots_max, TILE, TILE), BF16),
            vmem((slots_max + 1, TILE, TILE), BF16),
            vmem((n_cb, TILE, f), BF16),
            vmem(weight.shape, BF16),
            vmem((Z_HI, ch, hid), BF16),
            vmem((Z_HI, ch, hid), BF16),
            vmem((n_cb * TILE, n_cb * TILE), BF16),
            vmem((slots_max + 1, TILE, f), F32),
            vmem((n_blocks, block_rows, f), F32),
            vmem((n_blocks, n_x, ch, f), BF16),
            vmem((n_blocks, n_x, ch, f), BF16),
            vmem((n_blocks, n_x, ch, f), BF16),
            vmem((Z_HI, ch, f), F32),
            vmem((Z_HI, plane, ch, f), BF16),
            vmem((Z_HI, ch, f), BF16),
            vmem((Z_HI, ch, f), BF16),
            vmem((n_blocks, n_x, CORES, ch, f), BF16),
            vmem((n_cb * TILE, f), F32),
            vmem((n_row, zc, f), BF16),
            vmem((n_row, zc, f), BF16),
            vmem((zc, f), BF16),
            vmem((CORES, plane, piece, TILE), F32),
            vmem((plane, piece, TILE), F32),
            vmem((plane, piece, TILE), F32),
            vmem((n_row, piece, TILE), F32),
            vmem((CORES, plane, piece, TILE), F32),
            dma((7,)),
            dma((4,)),
            dma((2,)),
            dma,
            dma((n_blocks,)),
            dma,
            dma((Z_HI, 2)),
            dma,
            dma((Z_HI, 2)),
            dma,
            dma((Z_HI, 2, n_y)),
            dma,
            dma((Z_HI, n_y)),
            dma((2,)),
            dma((2,)),
            dma((2,)),
            dma((2,)),
            dma((2,)),
            dma((2,)),
        ],
        compiler_params=pltpu.CompilerParams(
            collective_id=0, has_side_effects=True, vmem_limit_bytes=40 * 1024 * 1024
        ),
        name="graph_layer",
    )(table, tile_cols[0, 0], *operands)
    weight_grad = wg.reshape(CORES, f, TILE).transpose(1, 0, 2).reshape(f, hid)
    return act, ig[None], weight_grad


def solution(mesh):
    in_specs = (
        P("row", ("col", "depth"), None, None, None),
        P("row", ("col", "depth"), None),
        P("row", ("col", "depth"), None),
        P("row", ("col", "depth")),
        P(("col", "depth"), None),
        P(),
        P(("row", "col", "depth"), None),
    )
    out_specs = (P(("row", "col", "depth"), None), P(("col", "depth"), "row", None), P())
    return jax.shard_map(local, mesh=mesh, in_specs=in_specs, out_specs=out_specs, check_vma=False)
```

time: 78.1 us -> 62.9 us (0.81)
  Pallas kernels: 69.7 us -> 57.9 us
  local copies, waits for them, and re-layouts: 6.01 us -> 2.54 us
    pallas_call x1, Pallas kernels: 69.7 us -> 57.9 us  [local(): pl.pallas_call(functools.partial(kernel, sizes), out_shape=(vmem((ch, hid...]
    unnamed x10 -> x4, local copies, waits for them, and re-layouts: 5.34 us -> 1.88 us
where the time goes in v2:
time: 62.9 us; the launch traced here: 62.5 us
  Pallas kernels  57.9 us (92%)
  local copies, waits for them, and re-layouts  2.54 us (4%)
  between operations  1.3 us (2%)
  other arithmetic  0.77 us (1%)
    pallas_call x1, Pallas kernels, local(): pl.pallas_call(functools.partial(kernel, sizes), out_shape=(vmem((ch, hid...  57.9 us
    unnamed x4, local copies, waits for them, and re-layouts  1.88 us

profile of v2, /device:TPU:1, one launch (start us, length us, event | category | flops | bytes accessed | tf_op | source)
XLA Modules:
  0.0 62.5 jit_solution(7387206059453729266)
XLA Ops:
  1.3 0.7 %compare_select_fusion = s32[64]{0:T(128)S(1)} fusion(s32[1,1,64]{2,1,0:T(1,128)} %param.8, s32[]{:T(128)} %bitcast.16, s32[1,1,64]{2,1,0:T(1,128)} %param.9), kind=kLoop, calls=%fused_computation.3 | loop fusion | flops 256 | bytes 772 | tf_op jit(solution)/shard_map/jit(_where)/select_n | solution.py:300
  2.0 0.1 select_reduce_fusion.table
  2.0 0.0 copy-start
  2.1 0.6 %copy-done = s32[1,1,64]{2,1,0:T(1,128)S(1)} copy-done((s32[1,1,64]{2,1,0:T(1,128)S(1)}, s32[1,1,64]{2,1,0:T(1,128)}, u32[]{:S(2)}) %copy-start) | copy-done | bytes 280
  2.7 57.9 %graph_layer.1 = (bf16[80,256]{1,0:T(8,128)(2,1)S(1)}, bf16[80,128]{1,0:T(8,128)(2,1)S(1)}, f32[2,16,8,128]{3,2,1,0:T(8,128)S(1)}) custom-call(s32[200]{0:T(256)S(1)} %select_reduce_fusion.table, s32[64]{0:T(128)S(1)} %bitcast.18, bf16[1,1,64,128,128]{4,3,2,1,0:T(8,128)(2,1)} %vals_in.1, bf16[5,128,128]{2,1,0:T(8,128)(2,1)} %bitcast.19, ...), custom_call_target="tpu_custom_call" | custom-call | tf_op jit(solution)/shard_map/graph_layer/pallas_call | solution.py:313
  60.6 0.6 copy.17
  61.3 0.6 copy.18
  61.9 0.7 %copy.14 = f32[2,16,8,128]{3,2,0,1:T(8,128)} copy(f32[2,16,8,128]{3,2,1,0:T(8,128)S(1)} %get-tuple-element.8) | data formatting | bytes 262144 | tf_op jit(solution)/shard_map/reshape | solution.py:375
Async XLA Ops:
  2.0 0.7 %copy-start = (s32[1,1,64]{2,1,0:T(1,128)S(1)}, s32[1,1,64]{2,1,0:T(1,128)}, u32[]{:S(2)}) copy-start(s32[1,1,64]{2,1,0:T(1,128)} %param.9) | copy-start | bytes 772

commit v3 on v2

--- a/solution.py
+++ b/solution.py
@@ -10,16 +10,17 @@
 
 TILE = 128
 Z_HI = 2
+LOADS = 8
 CORES = 2
 BF16 = jnp.bfloat16
 F32 = jnp.float32
 
 
 def kernel(
-    sizes, table, cols, vals_in, feat_in, w_in, cot_in, act_out, ig_out, wg_out,
-    vals, valst, feat, w, cot, act, dense, prod, part, sb, rb, qs, own, slots, zsend, zrecv, g, acc,
-    xs, xr, ig, wt, wr, wslots, wz, wo,
-    load_sem, out_sem, csem, s1s, s1r, s2s, s2r, zs, zr, ga_s, ga_r, gc_s, gc_r,
+    sizes, count_s, rows_in, cols_in, vals_in, feat_in, w_in, cot_in, act_out, ig_out, wg_out,
+    rows_s, cols_s, places, table, vals, valst, feat, w, cot, act, dense, prod, part, sb, rb, qs, own, slots, zsend, zrecv, g, acc,
+    xs, xr, wt, wr, wslots, wz, wo,
+    slot_sem, table_sem, load_sem, csem, s1s, s1r, s2s, s2r, zs, zr, ga_s, ga_r, gc_s, gc_r,
     xsem, w1, w2, w3, w5, w6,
 ):
     n_row, n_y, n_x, ch, n_cb, block_tiles, slots_max = sizes
@@ -46,8 +47,12 @@
     offsets = [(dy, dx) for dy in range(n_y) for dx in range(n_x) if (dy, dx) != (0, 0)]
     hops = lambda o: (min(o[0], n_y - o[0]), min(o[1], n_x - o[1]))
     offsets.sort(key=lambda o: (-sum(hops(o)), abs(hops(o)[0] - hops(o)[1]), o[0] + o[1]))
-    first = ch // 32 * 16 + ch // 16 % 2 * 16
-    pieces = [pl.ds(0, first), pl.ds(first, ch - first)]
+    long = (ch // 16 + 1) // 2 * 16
+    short = ch - long
+    pieces = [
+        [pl.ds(0, short), pl.ds(short, long)],
+        [pl.ds(0, long), pl.ds(long, short)],
+    ]
     units = [(phase, half) for phase in range(Z_HI) for half in range(2)]
     strides = sorted(range(1, n_row), key=lambda dz: -abs(2 * dz - n_row))
 
@@ -59,6 +64,25 @@
 
     def wait(ref, sem):
         pltpu.make_async_copy(ref, ref, sem).wait()
+
+    slot_loads = [
+        pltpu.make_async_copy(rows_in, rows_s, slot_sem.at[0]),
+        pltpu.make_async_copy(cols_in, cols_s, slot_sem.at[1]),
+    ]
+    part_slots = slots_max // LOADS
+    value_loads = []
+    for q in range(LOADS):
+        span = pl.ds(q * part_slots, part_slots)
+        value_loads.append(
+            pltpu.make_async_copy(vals_in.at[0, 0, span], vals.at[span], load_sem.at[q])
+        )
+    feat_load = pltpu.make_async_copy(feat_in, feat, load_sem.at[LOADS])
+    late_loads = [
+        pltpu.make_async_copy(cot_in, cot.at[zh], load_sem.at[LOADS + 1]),
+        pltpu.make_async_copy(w_in, w, load_sem.at[LOADS + 2]),
+    ]
+    for load in slot_loads + [feat_load] + value_loads + late_loads:
+        load.start()
 
     barrier = pltpu.get_barrier_semaphore()
     peers = [sibling, partner]
@@ -67,64 +91,78 @@
     for peer in peers:
         pl.semaphore_signal(barrier, inc=1, device_id=peer, device_id_type=pl.DeviceIdType.MESH)
 
-    quarter = slots_max // 4
-    loads = [pltpu.make_async_copy(feat_in, feat, load_sem.at[0])]
-    for q in range(4):
-        span = pl.ds(q * quarter, quarter)
-        loads.append(pltpu.make_async_copy(vals_in.at[0, 0, span], vals.at[span], load_sem.at[1 + q]))
-    late_loads = [
-        pltpu.make_async_copy(cot_in, cot.at[zh], load_sem.at[5]),
-        pltpu.make_async_copy(w_in, w, load_sem.at[6]),
-    ]
-    for load in loads + late_loads:
-        load.start()
-
     valst[slots_max] = jnp.zeros((TILE, TILE), BF16)
     prod[slots_max] = jnp.zeros((TILE, TILE), F32)
-    for load in loads:
+
+    for load in slot_loads:
         load.wait()
-
-    def multiply(t, carry):
-        for u in range(4):
-            s = 4 * t + u
-            prod[s] = jnp.dot(vals[s], feat[cols[s]], preferred_element_type=F32)
-        return carry
-
-    lax.fori_loop(0, slots_max // 4, multiply, 0)
+    count = count_s[0, 0]
+    place = lax.broadcasted_iota(jnp.int32, places.shape, 0) * TILE
+    place = place + lax.broadcasted_iota(jnp.int32, places.shape, 1)
+
+    def fill(t, found):
+        for u in range(LOADS):
+            s = t * LOADS + u
+            key = jnp.where(s < count, rows_s[0, 0, s] * n_cb + cols_s[0, 0, s], -1)
+            found = jnp.where(place == key, s, found)
+        return found
+
+    places[...] = lax.fori_loop(
+        0, slots_max // LOADS, fill, jnp.full(places.shape, slots_max, jnp.int32)
+    )
+    table_copy = pltpu.make_async_copy(places, table, table_sem)
+    table_copy.start()
+
+    def slot_at(p):
+        return table[lax.div(p, TILE), lax.rem(p, TILE)]
+
+    feat_load.wait()
+
+    for q in range(LOADS):
+        value_loads[q].wait()
+
+        def multiply(t, carry):
+            for u in range(4):
+                s = q * part_slots + 4 * t + u
+                prod[s] = jnp.dot(vals[s], feat[cols_s[0, 0, s]], preferred_element_type=F32)
+            return carry
+
+        lax.fori_loop(0, part_slots // 4, multiply, 0)
+    table_copy.wait()
 
     def chunk(b, xx, cc):
         return part[b, pl.ds(pl.multiple_of((xx * CORES + cc) * ch, 16), ch), :]
 
-    def gather_products(b, carry):
+    def gather_products(j, carry):
+        b = lax.div(j, n_y) * n_y + lax.rem(y + j, n_y)
         for i in range(block_tiles):
             at = (b * block_tiles + i) * n_cb
-            total = prod[table[at]]
+            total = prod[slot_at(at)]
             for c in range(1, n_cb):
-                total = total + prod[table[at + c]]
+                total = total + prod[slot_at(at + c)]
             part[b, i * TILE : (i + 1) * TILE, :] = total
         for xx in range(n_x):
             sb[b, xx] = chunk(b, xx, other).astype(BF16)
+        send(sb.at[b], rb.at[b], s1s, s1r.at[b], sibling)
         return carry
 
+    pl.semaphore_wait(barrier, len(peers))
     lax.fori_loop(0, n_blocks, gather_products, 0)
-    pl.semaphore_wait(barrier, len(peers))
-    for b in range(n_blocks):
-        send(sb.at[b], rb.at[b], s1s, s1r.at[b], sibling)
     for load in late_loads:
         load.wait()
     send(cot.at[zh], cot.at[zh], csem.at[0], csem.at[1], partner)
 
     for phase in range(Z_HI):
 
-        def pair(yy, carry):
-            b = phase * n_y + yy
+        def pair(i, carry):
+            b = phase * n_y + lax.rem(y + i, n_y)
             wait(rb.at[b], s1r.at[b])
             for xx in range(n_x):
                 qs[b, xx] = (chunk(b, xx, core) + rb[b, xx].astype(F32)).astype(BF16)
             return carry
 
         lax.fori_loop(0, n_y, pair, 0)
-        for half, rows in enumerate(pieces):
+        for half, rows in enumerate(pieces[phase]):
             for dy, dx in offsets:
                 yy, xx, device = in_plane(dy, dx)
                 send(
@@ -135,7 +173,7 @@
         own[phase] = chunk(b, x, core) + rb[b, x].astype(F32)
 
     for phase, half in units:
-        rows = pieces[half]
+        rows = pieces[phase][half]
         wait(slots.at[phase, pl.ds(1, plane - 1), rows], s2r.at[phase, half])
         total = own[phase, rows]
         for k in range(1, plane):
@@ -152,7 +190,7 @@
     wait(cot.at[z_other], csem.at[1])
 
     for phase, half in units:
-        rows = pieces[half]
+        rows = pieces[phase][half]
         wait(zrecv.at[phase, rows], zr.at[phase, half])
         agg = (zsend[phase, rows].astype(F32) + zrecv[phase, rows].astype(F32)).astype(BF16)
         pre = jnp.dot(agg, w[...], preferred_element_type=F32)
@@ -164,24 +202,26 @@
         )
         mine = g.at[phase * n_y + y, x, core, rows]
         mine[...] = grad_agg.astype(BF16)
-        for dy, dx in offsets:
-            send(mine, mine, ga_s, ga_r.at[phase, half, dy], in_plane(dy, dx)[2])
-        act[phase, rows] = (pre * sig).astype(BF16)
+        if (phase, half) != units[-1]:
+            for dy, dx in offsets:
+                send(mine, mine, ga_s, ga_r.at[phase, half, dy], in_plane(dy, dx)[2])
         terms = lax.dot_general(
             agg, grad_pre, (((0,), (0,)), ((), ())), preferred_element_type=F32
         )
         for lane in range(CORES):
             term = terms[:, lane * TILE : (lane + 1) * TILE].reshape(wt.shape[1:])
-            wt[lane] = term if (phase, half) == (0, 0) else wt[lane] + term
+            wt[lane] = term if (phase, half) == units[0] else wt[lane] + term
+        act[phase, rows] = (pre * sig).astype(BF16)
+
     send(wt.at[other], wr, w1.at[0], w1.at[1], sibling)
-    act_copy = pltpu.make_async_copy(act.at[zh], act_out, out_sem.at[0])
-    act_copy.start()
-
+    act_out[...] = act[zh]
     wait(wr, w1.at[1])
     wt[core] = wt[core] + wr[...]
     for dy, dx in offsets:
         yy, xx, device = in_plane(dy, dx)
         send(wt.at[core, yy * n_x + xx], wslots.at[dy * n_x + dx], w2.at[0], w2.at[1], device)
+    for dy, dx in offsets:
+        send(mine, mine, ga_s, ga_r.at[phase, half, dy], in_plane(dy, dx)[2])
 
     acc[...] = jnp.zeros_like(acc)
 
@@ -196,7 +236,7 @@
                 dy, b = source(i)
                 group = g.at[b, pl.ds(0, n_x), core]
 
-                for half, rows in enumerate(pieces):
+                for half, rows in enumerate(pieces[phase]):
 
                     @pl.when(dy == 0)
                     def _():
@@ -214,7 +254,7 @@
                 wait(g.at[b, pl.ds(0, n_x), other], gc_r.at[phase, dy])
                 for c in range(n_cb):
                     for t in range(block_tiles):
-                        slot = table[(b * block_tiles + t) * n_cb + c]
+                        slot = slot_at((b * block_tiles + t) * n_cb + c)
                         dense[c * TILE : (c + 1) * TILE, t * TILE : (t + 1) * TILE] = valst[slot]
                 grad = g[b].reshape(block_tiles * TILE, TILE)
                 acc[...] += jnp.dot(dense[...], grad, preferred_element_type=F32)
@@ -255,15 +295,10 @@
     wait(xr.at[pl.ds(1, n_row - 1)], xsem.at[1])
     for k in range(1, n_row):
         total = total + xr[k].astype(F32)
-    ig[...] = total.astype(BF16)
-    ig_copy = pltpu.make_async_copy(ig, ig_out, out_sem.at[1])
-    ig_copy.start()
+    ig_out[...] = total.astype(BF16)
     wait(wo.at[other], w6.at[1])
-    wg_copies = [
-        pltpu.make_async_copy(wo.at[c], wg_out.at[c], out_sem.at[2 + c]) for c in range(CORES)
-    ]
-    for copy in wg_copies:
-        copy.start()
+    for c in range(CORES):
+        wg_out[c] = wo[c].reshape(TILE, TILE)
 
     wait(sb, s1s)
     wait(cot.at[zh], csem.at[0])
@@ -277,7 +312,19 @@
     wait(wo.at[core, pl.ds(0, plane - 1)], w5.at[0])
     wait(wo.at[core], w6.at[0])
     wait(xr.at[pl.ds(1, n_row - 1)], xsem.at[0])
-    for copy in [act_copy, ig_copy] + wg_copies:
+
+
+def deliver(act, ig, wg, act_out, ig_out, wg_out, sem):
+    copies = [
+        pltpu.make_async_copy(act, act_out, sem.at[0]),
+        pltpu.make_async_copy(ig, ig_out, sem.at[1]),
+    ]
+    for c in range(CORES):
+        lanes = pl.ds(c * TILE, TILE)
+        copies.append(pltpu.make_async_copy(wg.at[c], wg_out.at[:, lanes], sem.at[2 + c]))
+    for copy in copies:
+        copy.start()
+    for copy in copies:
         copy.wait()
 
 
@@ -290,24 +337,19 @@
     n_blocks = n_col
     block_rows = n_depth * ch
     block_tiles = block_rows // TILE
-    n_tiles = n_blocks * block_tiles
     slots_max = tile_values.shape[2]
     plane = n_x * n_y
     zc = features.shape[0] // n_row
     piece = f // plane
 
-    slot = jnp.arange(slots_max, dtype=jnp.int32)
-    key = jnp.where(slot < tile_count[0, 0], tile_rows[0, 0] * n_cb + tile_cols[0, 0], -1)
-    where_at = jnp.arange(n_tiles * n_cb, dtype=jnp.int32)
-    table = jnp.min(
-        jnp.where(key[:, None] == where_at[None, :], slot[:, None], slots_max), axis=0
-    )
-
     sizes = (n_row, n_y, n_x, ch, n_cb, block_tiles, slots_max)
     vmem, dma = pltpu.VMEM, pltpu.SemaphoreType.DMA
     operands = [
         pltpu.with_memory_space_constraint(a, pltpu.HBM)
-        for a in (tile_values, features.reshape(n_cb, TILE, f), weight, cotangent)
+        for a in (
+            tile_rows, tile_cols, tile_values, features.reshape(n_cb, TILE, f),
+            weight, cotangent,
+        )
     ]
     anywhere = pl.BlockSpec(memory_space=pl.ANY)
     act, ig, wg = pl.pallas_call(
@@ -315,12 +357,16 @@
         out_shape=(
             vmem((ch, hid), BF16),
             vmem((zc, f), BF16),
-            vmem((CORES, plane, piece, TILE), F32),
+            vmem((CORES, f, TILE), F32),
         ),
-        in_specs=[pl.BlockSpec(memory_space=pltpu.SMEM)] * 2
-        + [pl.BlockSpec(memory_space=pltpu.HBM)] * 4,
-        out_specs=(anywhere,) * 3,
+        in_specs=[pl.BlockSpec(memory_space=pltpu.SMEM)]
+        + [pl.BlockSpec(memory_space=pltpu.HBM)] * 6,
+        out_specs=(pl.BlockSpec(memory_space=pltpu.VMEM),) * 3,
         scratch_shapes=[
+            pltpu.SMEM(tile_rows.shape, jnp.int32),
+            pltpu.SMEM(tile_cols.shape, jnp.int32),
+            vmem((8, TILE), jnp.int32),
+            pltpu.SMEM((8, TILE), jnp.int32),
             vmem((slots_max, TILE, TILE), BF16),
             vmem((slots_max + 1, TILE, TILE), BF16),
             vmem((n_cb, TILE, f), BF16),
@@ -341,14 +387,14 @@
             vmem((n_cb * TILE, f), F32),
             vmem((n_row, zc, f), BF16),
             vmem((n_row, zc, f), BF16),
-            vmem((zc, f), BF16),
             vmem((CORES, plane, piece, TILE), F32),
             vmem((plane, piece, TILE), F32),
             vmem((plane, piece, TILE), F32),
             vmem((n_row, piece, TILE), F32),
             vmem((CORES, plane, piece, TILE), F32),
-            dma((7,)),
-            dma((4,)),
+            dma((2,)),
+            dma,
+            dma((LOADS + 3,)),
             dma((2,)),
             dma,
             dma((n_blocks,)),
@@ -371,8 +417,19 @@
             collective_id=0, has_side_effects=True, vmem_limit_bytes=40 * 1024 * 1024
         ),
         name="graph_layer",
-    )(table, tile_cols[0, 0], *operands)
-    weight_grad = wg.reshape(CORES, f, TILE).transpose(1, 0, 2).reshape(f, hid)
+    )(tile_count, *operands)
+    act, ig, weight_grad = pl.pallas_call(
+        deliver,
+        out_shape=(
+            jax.ShapeDtypeStruct((ch, hid), BF16),
+            jax.ShapeDtypeStruct((zc, f), BF16),
+            jax.ShapeDtypeStruct((f, hid), F32),
+        ),
+        in_specs=[pl.BlockSpec(memory_space=pltpu.VMEM)] * 3,
+        out_specs=(pl.BlockSpec(memory_space=pltpu.HBM),) * 3,
+        scratch_shapes=[dma((2 + CORES,))],
+        name="deliver",
+    )(*[pltpu.with_memory_space_constraint(a, pltpu.VMEM) for a in (act, ig, wg)])
     return act, ig[None], weight_grad
 
 

time: 62.9 us -> 59 us (0.938)
  local copies, waits for them, and re-layouts: 2.54 us -> 0 us
  other arithmetic: 0.77 us -> 0 us
    unnamed x4 -> x0, local copies, waits for them, and re-layouts: 1.88 us -> none
    pallas_call x1, Pallas kernels: 57.9 us -> 56.9 us  [local(): pl.pallas_call(functools.partial(kernel, sizes), out_shape=(vmem((ch, hid...]
    pallas_call x0 -> x1, Pallas kernels: none -> 0.71 us  [local(): pl.pallas_call(deliver, out_shape=(jax.ShapeDtypeStruct((ch, hid), BF16),...]
    select_n x1 -> x0, other arithmetic: 0.68 us -> none  [local(): jnp.where(slot < tile_count[0, 0], tile_rows[0, 0] * n_cb + tile_cols[0,...]
    reshape x1 -> x0, local copies, waits for them, and re-layouts: 0.66 us -> none  [local(): weight_grad = wg.reshape(CORES, f, TILE).transpose(1, 0, 2).reshape(f, hid)]
where the time goes in v3:
time: 59 us; the launch traced here: 58.9 us
  Pallas kernels  57.6 us (98%)
  between operations  1.29 us (2%)
    pallas_call x1, Pallas kernels, local(): pl.pallas_call(functools.partial(kernel, sizes), out_shape=(vmem((ch, hid...  56.9 us

profile of v3, /device:TPU:1, one launch (start us, length us, event | category | flops | bytes accessed | tf_op | source)
XLA Modules:
  0.0 58.9 jit_solution(7297550286007323525)
XLA Ops:
  1.3 56.9 %graph_layer.1 = (bf16[80,256]{1,0:T(8,128)(2,1)S(1)}, bf16[80,128]{1,0:T(8,128)(2,1)S(1)}, f32[2,128,128]{2,1,0:T(8,128)S(1)}) custom-call(s32[1,1]{1,0:T(1,128)S(6)} %copy.10.count_s, s32[1,1,64]{2,1,0:T(1,128)} %rows_in.1, s32[1,1,64]{2,1,0:T(1,128)} %cols_in.1, bf16[1,1,64,128,128]{4,3,2,1,0:T(8,128)(2,1)} %vals_in.1, bf16[5,128,128]{2,1,0:T(8,128)(2,1)} %bitcast.2, ...), custom_call_target="tpu_custom_call" | custom-call | tf_op jit(solution)/shard_map/graph_layer/pallas_call | solution.py:355
  58.1 0.7 %deliver.1 = (bf16[80,256]{1,0:T(8,128)(2,1)}, bf16[80,128]{1,0:T(8,128)(2,1)}, f32[128,256]{1,0:T(8,128)}) custom-call(bf16[80,256]{1,0:T(8,128)(2,1)S(1)} %get-tuple-element.9.act, bf16[80,128]{1,0:T(8,128)(2,1)S(1)} %get-tuple-element.10.ig, f32[2,128,128]{2,1,0:T(8,128)S(1)} %get-tuple-element.11.wg), custom_call_target="tpu_custom_call" | custom-call | tf_op jit(solution)/shard_map/deliver/pallas_call | solution.py:421

commit v4 on v3

--- a/solution.py
+++ b/solution.py
@@ -172,6 +172,17 @@
         b = phase * n_y + y
         own[phase] = chunk(b, x, core) + rb[b, x].astype(F32)
 
+    def turn(first, last):
+        def step(t, carry):
+            for u in range(4):
+                valst[4 * t + u] = vals[4 * t + u].T
+            return carry
+
+        lax.fori_loop(first // 4, last // 4, step, 0)
+
+    half_slots = slots_max // 8 * 4
+    turn(0, half_slots)
+
     for phase, half in units:
         rows = pieces[phase][half]
         wait(slots.at[phase, pl.ds(1, plane - 1), rows], s2r.at[phase, half])
@@ -181,12 +192,9 @@
         zsend[phase, rows] = total.astype(BF16)
         mine = zsend.at[phase, rows]
         send(mine, zrecv.at[phase, rows], zs, zr.at[phase, half], partner)
-
-    def turn(t, carry):
-        valst[t] = vals[t].T
-        return carry
-
-    lax.fori_loop(0, slots_max, turn, 0)
+        if (phase, half) == units[0]:
+            turn(half_slots, slots_max)
+
     wait(cot.at[z_other], csem.at[1])
 
     for phase, half in units:
@@ -251,11 +259,11 @@
             @pl.when(i > 0)
             def _():
                 dy, b = source(i - 1)
-                wait(g.at[b, pl.ds(0, n_x), other], gc_r.at[phase, dy])
                 for c in range(n_cb):
                     for t in range(block_tiles):
                         slot = slot_at((b * block_tiles + t) * n_cb + c)
                         dense[c * TILE : (c + 1) * TILE, t * TILE : (t + 1) * TILE] = valst[slot]
+                wait(g.at[b, pl.ds(0, n_x), other], gc_r.at[phase, dy])
                 grad = g[b].reshape(block_tiles * TILE, TILE)
                 acc[...] += jnp.dot(dense[...], grad, preferred_element_type=F32)
 
@@ -273,10 +281,9 @@
         send(wz.at[row], wz.at[row], w3.at[0], w3.at[1], in_row(dz)[1])
 
     gather(1)
-    for d in range(n_row):
-        xs[d] = acc[d * zc : (d + 1) * zc, :].astype(BF16)
     for dz in strides:
         rr, device = in_row(dz)
+        xs[rr] = acc[pl.ds(pl.multiple_of(rr * zc, 16), zc), :].astype(BF16)
         send(xs.at[rr], xr.at[dz], xsem.at[0], xsem.at[1], device)
 
     wait(wz.at[pl.ds(0, n_row - 1)], w3.at[1])

time: 59 us -> 56.2 us (0.953)
  Pallas kernels: 57.6 us -> 54.4 us
    pallas_call x1, Pallas kernels: 56.9 us -> 53.7 us  [local(): pl.pallas_call(functools.partial(kernel, sizes), out_shape=(vmem((ch, hid...]
where the time goes in v4:
time: 56.2 us; the launch traced here: 55.7 us
  Pallas kernels  54.4 us (97%)
  between operations  1.29 us (2%)
    pallas_call x1, Pallas kernels, local(): pl.pallas_call(functools.partial(kernel, sizes), out_shape=(vmem((ch, hid...  53.7 us

profile of v4, /device:TPU:1, one launch (start us, length us, event | category | flops | bytes accessed | tf_op | source)
XLA Modules:
  0.0 55.7 jit_solution(8098861465097225999)
XLA Ops:
  1.3 53.7 %graph_layer.1 = (bf16[80,256]{1,0:T(8,128)(2,1)S(1)}, bf16[80,128]{1,0:T(8,128)(2,1)S(1)}, f32[2,128,128]{2,1,0:T(8,128)S(1)}) custom-call(s32[1,1]{1,0:T(1,128)S(6)} %copy.10.count_s, s32[1,1,64]{2,1,0:T(1,128)} %rows_in.1, s32[1,1,64]{2,1,0:T(1,128)} %cols_in.1, bf16[1,1,64,128,128]{4,3,2,1,0:T(8,128)(2,1)} %vals_in.1, bf16[5,128,128]{2,1,0:T(8,128)(2,1)} %bitcast.2, ...), custom_call_target="tpu_custom_call" | custom-call | tf_op jit(solution)/shard_map/graph_layer/pallas_call | solution.py:362
  55.0 0.7 %deliver.1 = (bf16[80,256]{1,0:T(8,128)(2,1)}, bf16[80,128]{1,0:T(8,128)(2,1)}, f32[128,256]{1,0:T(8,128)}) custom-call(bf16[80,256]{1,0:T(8,128)(2,1)S(1)} %get-tuple-element.9.act, bf16[80,128]{1,0:T(8,128)(2,1)S(1)} %get-tuple-element.10.ig, f32[2,128,128]{2,1,0:T(8,128)S(1)} %get-tuple-element.11.wg), custom_call_target="tpu_custom_call" | custom-call | tf_op jit(solution)/shard_map/deliver/pallas_call | solution.py:428

commit v5 on v4

--- a/solution.py
+++ b/solution.py
@@ -180,8 +180,17 @@
 
         lax.fori_loop(first // 4, last // 4, step, 0)
 
-    half_slots = slots_max // 8 * 4
-    turn(0, half_slots)
+    turn(0, slots_max)
+
+    def spread_tiles(first, last):
+        def step(b, carry):
+            for c in range(n_cb):
+                for t in range(block_tiles):
+                    slot = slot_at((b * block_tiles + t) * n_cb + c)
+                    dense[b, c * TILE : (c + 1) * TILE, t * TILE : (t + 1) * TILE] = valst[slot]
+            return carry
+
+        lax.fori_loop(first, last, step, 0)
 
     for phase, half in units:
         rows = pieces[phase][half]
@@ -192,8 +201,8 @@
         zsend[phase, rows] = total.astype(BF16)
         mine = zsend.at[phase, rows]
         send(mine, zrecv.at[phase, rows], zs, zr.at[phase, half], partner)
-        if (phase, half) == units[0]:
-            turn(half_slots, slots_max)
+        done = units.index((phase, half))
+        spread_tiles(n_blocks * done // len(units), n_blocks * (done + 1) // len(units))
 
     wait(cot.at[z_other], csem.at[1])
 
@@ -238,38 +247,33 @@
             dy = i + lax.div(i, 2) * (5 - 2 * i)
             return dy, phase * n_y + lax.rem(y + n_y - dy, n_y)
 
-        def step(i, carry):
-            @pl.when(i < n_y)
-            def _():
-                dy, b = source(i)
-                group = g.at[b, pl.ds(0, n_x), core]
-
-                for half, rows in enumerate(pieces[phase]):
-
-                    @pl.when(dy == 0)
-                    def _():
-                        wait(slots.at[0, pl.ds(0, n_x - 1), rows], ga_r.at[phase, half, dy])
-
-                    @pl.when(dy != 0)
-                    def _():
-                        wait(g.at[b, pl.ds(0, n_x), core, rows], ga_r.at[phase, half, dy])
-
-                send(group, group, gc_s, gc_r.at[phase, dy], sibling)
-
-            @pl.when(i > 0)
-            def _():
-                dy, b = source(i - 1)
-                for c in range(n_cb):
-                    for t in range(block_tiles):
-                        slot = slot_at((b * block_tiles + t) * n_cb + c)
-                        dense[c * TILE : (c + 1) * TILE, t * TILE : (t + 1) * TILE] = valst[slot]
-                wait(g.at[b, pl.ds(0, n_x), other], gc_r.at[phase, dy])
-                grad = g[b].reshape(block_tiles * TILE, TILE)
-                acc[...] += jnp.dot(dense[...], grad, preferred_element_type=F32)
-
-            return carry
-
-        lax.fori_loop(0, n_y + 1, step, 0)
+        def pass_on(i, carry):
+            dy, b = source(i)
+            group = g.at[b, pl.ds(0, n_x), core]
+            for half, rows in enumerate(pieces[phase]):
+
+                @pl.when(dy == 0)
+                def _():
+                    wait(slots.at[0, pl.ds(0, n_x - 1), rows], ga_r.at[phase, half, dy])
+
+                @pl.when(dy != 0)
+                def _():
+                    wait(g.at[b, pl.ds(0, n_x), core, rows], ga_r.at[phase, half, dy])
+
+            send(group, group, gc_s, gc_r.at[phase, dy], sibling)
+            return carry
+
+        def multiply(i, carry):
+            dy, b = source(i)
+            wait(g.at[b, pl.ds(0, n_x), other], gc_r.at[phase, dy])
+            grad = g[b].reshape(block_tiles * TILE, TILE)
+            for c in range(n_cb):
+                at = pl.ds(c * TILE, TILE)
+                acc[at, :] += jnp.dot(dense[b, at, :], grad, preferred_element_type=F32)
+            return carry
+
+        lax.fori_loop(0, n_y, pass_on, 0)
+        lax.fori_loop(0, n_y, multiply, 0)
 
     gather(0)
     wait(wslots.at[pl.ds(1, plane - 1)], w2.at[1])
@@ -380,7 +384,7 @@
             vmem(weight.shape, BF16),
             vmem((Z_HI, ch, hid), BF16),
             vmem((Z_HI, ch, hid), BF16),
-            vmem((n_cb * TILE, n_cb * TILE), BF16),
+            vmem((n_blocks, n_cb * TILE, block_rows), BF16),
             vmem((slots_max + 1, TILE, f), F32),
             vmem((n_blocks, block_rows, f), F32),
             vmem((n_blocks, n_x, ch, f), BF16),

time: 56.2 us -> 55.7 us (level)
  no operation moved by 1% of the time
where the time goes in v5:
time: 55.7 us; the launch traced here: 55.6 us
  Pallas kernels  54.3 us (97%)
  between operations  1.29 us (2%)
    pallas_call x1, Pallas kernels, local(): pl.pallas_call(functools.partial(kernel, sizes), out_shape=(vmem((ch, hid...  53.6 us

profile of v5, /device:TPU:1, one launch (start us, length us, event | category | flops | bytes accessed | tf_op | source)
XLA Modules:
  0.0 55.6 jit_solution(6652991960767114715)
XLA Ops:
  1.3 53.6 %graph_layer.1 = (bf16[80,256]{1,0:T(8,128)(2,1)S(1)}, bf16[80,128]{1,0:T(8,128)(2,1)S(1)}, f32[2,128,128]{2,1,0:T(8,128)S(1)}) custom-call(s32[1,1]{1,0:T(1,128)S(6)} %copy.10.count_s, s32[1,1,64]{2,1,0:T(1,128)} %rows_in.1, s32[1,1,64]{2,1,0:T(1,128)} %cols_in.1, bf16[1,1,64,128,128]{4,3,2,1,0:T(8,128)(2,1)} %vals_in.1, bf16[5,128,128]{2,1,0:T(8,128)(2,1)} %bitcast.2, ...), custom_call_target="tpu_custom_call" | custom-call | tf_op jit(solution)/shard_map/graph_layer/pallas_call | solution.py:366
  54.9 0.7 %deliver.1 = (bf16[80,256]{1,0:T(8,128)(2,1)}, bf16[80,128]{1,0:T(8,128)(2,1)}, f32[128,256]{1,0:T(8,128)}) custom-call(bf16[80,256]{1,0:T(8,128)(2,1)S(1)} %get-tuple-element.9.act, bf16[80,128]{1,0:T(8,128)(2,1)S(1)} %get-tuple-element.10.ig, f32[2,128,128]{2,1,0:T(8,128)S(1)} %get-tuple-element.11.wg), custom_call_target="tpu_custom_call" | custom-call | tf_op jit(solution)/shard_map/deliver/pallas_call | solution.py:432

commit v6 on v5

--- a/solution.py
+++ b/solution.py
@@ -133,8 +133,11 @@
     def chunk(b, xx, cc):
         return part[b, pl.ds(pl.multiple_of((xx * CORES + cc) * ch, 16), ch), :]
 
+    def block_of(j):
+        return lax.div(j, n_y) * n_y + lax.rem(y + j + n_y // 2, n_y)
+
     def gather_products(j, carry):
-        b = lax.div(j, n_y) * n_y + lax.rem(y + j, n_y)
+        b = block_of(j)
         for i in range(block_tiles):
             at = (b * block_tiles + i) * n_cb
             total = prod[slot_at(at)]
@@ -143,11 +146,19 @@
             part[b, i * TILE : (i + 1) * TILE, :] = total
         for xx in range(n_x):
             sb[b, xx] = chunk(b, xx, other).astype(BF16)
+        return carry
+
+    def to_sibling(j, carry):
+        b = block_of(j)
         send(sb.at[b], rb.at[b], s1s, s1r.at[b], sibling)
         return carry
 
+    lax.fori_loop(0, n_y, gather_products, 0)
     pl.semaphore_wait(barrier, len(peers))
-    lax.fori_loop(0, n_blocks, gather_products, 0)
+    lax.fori_loop(0, n_y, to_sibling, 0)
+    lax.fori_loop(
+        n_y, n_blocks, lambda j, carry: to_sibling(j, gather_products(j, carry)), 0
+    )
     for load in late_loads:
         load.wait()
     send(cot.at[zh], cot.at[zh], csem.at[0], csem.at[1], partner)
@@ -155,14 +166,26 @@
     for phase in range(Z_HI):
 
         def pair(i, carry):
-            b = phase * n_y + lax.rem(y + i, n_y)
+            b = block_of(phase * n_y + i)
             wait(rb.at[b], s1r.at[b])
             for xx in range(n_x):
                 qs[b, xx] = (chunk(b, xx, core) + rb[b, xx].astype(F32)).astype(BF16)
+            dy = lax.rem(i + n_y // 2, n_y)
+            rows = pieces[phase][0]
+            for dx in range(n_x):
+                _, xx, device = in_plane(dy, dx)
+
+                @pl.when(dy + dx > 0)
+                def _():
+                    send(
+                        qs.at[b, xx, rows], slots.at[phase, dy * n_x + dx, rows],
+                        s2s, s2r.at[phase, 0], device,
+                    )
+
             return carry
 
         lax.fori_loop(0, n_y, pair, 0)
-        for half, rows in enumerate(pieces[phase]):
+        for half, rows in list(enumerate(pieces[phase]))[1:]:
             for dy, dx in offsets:
                 yy, xx, device = in_plane(dy, dx)
                 send(

time: 55.7 us -> 56.2 us (level)
  no operation moved by 1% of the time
where the time goes in v6:
time: 56.2 us; the launch traced here: 56.1 us
  Pallas kernels  54.8 us (98%)
  between operations  1.29 us (2%)
    pallas_call x1, Pallas kernels, local(): pl.pallas_call(functools.partial(kernel, sizes), out_shape=(vmem((ch, hid...  54.1 us

profile of v6, /device:TPU:1, one launch (start us, length us, event | category | flops | bytes accessed | tf_op | source)
XLA Modules:
  0.0 56.1 jit_solution(7352045844607559966)
XLA Ops:
  1.3 54.1 %graph_layer.1 = (bf16[80,256]{1,0:T(8,128)(2,1)S(1)}, bf16[80,128]{1,0:T(8,128)(2,1)S(1)}, f32[2,128,128]{2,1,0:T(8,128)S(1)}) custom-call(s32[1,1]{1,0:T(1,128)S(6)} %copy.10.count_s, s32[1,1,64]{2,1,0:T(1,128)} %rows_in.1, s32[1,1,64]{2,1,0:T(1,128)} %cols_in.1, bf16[1,1,64,128,128]{4,3,2,1,0:T(8,128)(2,1)} %vals_in.1, bf16[5,128,128]{2,1,0:T(8,128)(2,1)} %bitcast.2, ...), custom_call_target="tpu_custom_call" | custom-call | tf_op jit(solution)/shard_map/graph_layer/pallas_call | solution.py:389
  55.4 0.7 %deliver.1 = (bf16[80,256]{1,0:T(8,128)(2,1)}, bf16[80,128]{1,0:T(8,128)(2,1)}, f32[128,256]{1,0:T(8,128)}) custom-call(bf16[80,256]{1,0:T(8,128)(2,1)S(1)} %get-tuple-element.9.act, bf16[80,128]{1,0:T(8,128)(2,1)S(1)} %get-tuple-element.10.ig, f32[2,128,128]{2,1,0:T(8,128)S(1)} %get-tuple-element.11.wg), custom_call_target="tpu_custom_call" | custom-call | tf_op jit(solution)/shard_map/deliver/pallas_call | solution.py:455
